TPU v7x, 32 devices: a whole 2x2x4 slice. The times are simulated.
32 devices in a mesh: groups: 2 (over y), outer: 2 (over x), inner: 4 (over z), head: 2 (over core).
Axes of the slice: x: 2, y: 2, z: 4, core: 2. Of those that a mesh axis runs over, the one named last changes fastest.
Arguments:
- queries: float32 [6144, 512], P(('groups', 'outer', 'inner'), 'head'), parts along dimension 0, may hold values from -5 to 5
- key_states: float32 [6144, 512], P(('groups', 'outer', 'inner'), 'head'), parts along dimension 0, may hold values from -5 to 5
- value_states: float32 [6144, 512], P(('groups', 'outer', 'inner'), 'head'), parts along dimension 0, may hold values from -5 to 5
- cotangent: bfloat16 [6144, 512], P(('groups', 'outer', 'inner'), 'head'), parts along dimension 0, may hold values from -5 to 5
Outputs:
- grad_queries: float32 [6144, 512], P(('groups', 'outer', 'inner'), 'head'), parts along dimension 0
- grad_keys: float32 [6144, 512], P(('groups', 'outer', 'inner'), 'head'), parts along dimension 0
- grad_values: float32 [6144, 512], P(('groups', 'outer', 'inner'), 'head'), parts along dimension 0
There are 2 independent parts, one for each index of `groups`. A program takes and returns all parts, laid end to end along the dimension named above; each array names one. Nothing has to cross between parts.
All inputs are finite; a program needn't handle non-finite values.
Results may differ from a plain program's by a relative error of at most 0.0003.
Values sent between devices are 32-bit elements; how exact they have to be, the bound alone decides.
A program may use at most 64 MiB of HBM per device.

v0:
```python
import math

import jax
import jax.numpy as jnp
from jax import lax
from jax.sharding import PartitionSpec as P

HD = 128
SEG = 384


def prefix(part, axis, combine, identity, reverse):
    count = lax.axis_size(axis)
    place = lax.axis_index(axis)
    ahead = count - 1 - place if reverse else place
    gathered = jax.tree.map(lambda a: lax.all_gather(a, axis), part)
    state = jax.tree.map(lambda a, e: jnp.zeros_like(a) + jnp.asarray(e, a.dtype), part, identity)

    def one(lap, state):
        source = count - 1 - lap if reverse else lap
        return combine(
            state, jax.tree.map(lambda a: lax.dynamic_index_in_dim(a, source, 0, False), gathered)
        )

    return lax.fori_loop(0, ahead, one, state)


def feature(inputs):
    return jax.nn.elu(inputs) + 1.0


def slope(inputs):
    return jnp.where(inputs > 0, 1.0, jnp.exp(jnp.minimum(inputs, 0.0)))


def add_pair(earlier, later):
    return (earlier[0] + later[0], earlier[1] + later[1])


def zero_pair(pair):
    return (jnp.zeros_like(pair[0]), jnp.zeros_like(pair[1]))


def entry_sums(pair):
    return prefix(pair, ("outer", "inner"), add_pair, zero_pair(pair), False)


def after_sums(pair):
    return prefix(pair, ("outer", "inner"), add_pair, zero_pair(pair), True)


def before_local(terms):
    running = jnp.cumsum(terms, axis=0)
    return jnp.concatenate([jnp.zeros_like(terms), running[:-1]], axis=0)


def after_local(terms):
    running = jnp.flip(jnp.cumsum(jnp.flip(terms, 0), axis=0), 0)
    return jnp.concatenate([running[1:], jnp.zeros_like(terms)], axis=0)


def shards(queries, key_states, value_states, cotangent):
    highest = lax.Precision.HIGHEST
    rows, columns = queries.shape
    heads_dev = columns // HD
    segments = rows // SEG
    shape = (segments, SEG, heads_dev, HD)
    query = queries.reshape(shape)
    keys = key_states.reshape(shape)
    values = value_states.reshape(shape)
    halfgrad = 0.5 * cotangent.astype(jnp.float32).reshape(shape)
    feat_query = feature(query)
    feat_key = feature(keys)
    seg_memory = jnp.einsum("sthi,sthj->shij", feat_key, values, precision=highest)
    seg_znorm = jnp.sum(feat_key, axis=1)
    before = entry_sums((jnp.sum(seg_memory, axis=0), jnp.sum(seg_znorm, axis=0)))
    memory = before[0][None] + before_local(seg_memory)
    znorm = before[1][None] + before_local(seg_znorm)
    numer = jnp.einsum("sthi,shij->sthj", feat_query, memory, precision=highest)
    raw_denom = jnp.einsum("sthi,shi->sth", feat_query, znorm, precision=highest)
    denom = jnp.maximum(raw_denom, 1.0)
    reading = numer / denom[..., None]
    grad_numer = halfgrad / denom[..., None]
    grad_denom = jnp.where(raw_denom > 1.0, -jnp.sum(halfgrad * reading, axis=-1) / denom, 0.0)
    grad_feat_query = (
        jnp.einsum("sthj,shij->sthi", grad_numer, memory, precision=highest)
        + grad_denom[..., None] * znorm[:, None]
    )
    seg_adjoint = jnp.einsum("sthi,sthj->shij", feat_query, grad_numer, precision=highest)
    seg_zadjoint = jnp.sum(feat_query * grad_denom[..., None], axis=1)
    after = after_sums((jnp.sum(seg_adjoint, axis=0), jnp.sum(seg_zadjoint, axis=0)))
    later_memory = after[0][None] + after_local(seg_adjoint)
    later_znorm = after[1][None] + after_local(seg_zadjoint)
    grad_feat_key = (
        jnp.einsum("sthj,shij->sthi", values, later_memory, precision=highest)
        + later_znorm[:, None]
    )
    grad_values_memory = jnp.einsum("sthi,shij->sthj", feat_key, later_memory, precision=highest)
    scale = 1.0 / math.sqrt(HD)
    scores = jnp.einsum("sthd,suhd->shtu", query, keys, precision=highest) * scale
    causal = jnp.arange(SEG)[:, None] >= jnp.arange(SEG)[None, :]
    scores = jnp.where(causal[None, None], scores, -jnp.inf)
    probs = jax.nn.softmax(scores, axis=-1)
    grad_probs = jnp.einsum("sthd,suhd->shtu", halfgrad, values, precision=highest)
    weighted = jnp.sum(grad_probs * probs, axis=-1)
    grad_scores = probs * (grad_probs - weighted[..., None]) * scale
    grad_query_local = jnp.einsum("shtu,suhd->sthd", grad_scores, keys, precision=highest)
    grad_key_local = jnp.einsum("shtu,sthd->suhd", grad_scores, query, precision=highest)
    grad_values_local = jnp.einsum("shtu,sthd->suhd", probs, halfgrad, precision=highest)
    grad_queries = grad_query_local + grad_feat_query * slope(query)
    grad_keys = grad_key_local + grad_feat_key * slope(keys)
    grad_values = grad_values_local + grad_values_memory
    return (
        grad_queries.reshape(rows, columns),
        grad_keys.reshape(rows, columns),
        grad_values.reshape(rows, columns),
    )


def solution(mesh):
    in_specs = (
        P(("groups", "outer", "inner"), "head"),
        P(("groups", "outer", "inner"), "head"),
        P(("groups", "outer", "inner"), "head"),
        P(("groups", "outer", "inner"), "head"),
    )
    out_specs = (
        P(("groups", "outer", "inner"), "head"),
        P(("groups", "outer", "inner"), "head"),
        P(("groups", "outer", "inner"), "head"),
    )
    return jax.shard_map(shards, mesh=mesh, in_specs=in_specs, out_specs=out_specs, check_vma=False)
```

profile of v0, /device:TPU:0, one launch (start us, length us, event | category | flops | bytes accessed | tf_op | source)
XLA Modules:
  0.0 120.2 jit_solution(2783565198340150914)
XLA Ops:
  7.2 0.9 copy-done
  8.2 2.6 %fusion.25 = f32[2,128,128]{2,1,0:T(8,128)} fusion(f32[384,256]{1,0:T(8,128)S(1)} %copy-done, f32[384,256]{1,0:T(8,128)} %param.9), kind=kOutput, calls=%fused_computation.50 | convolution fusion | flops 151388160 | bytes 917504 | tf_op jit(solution)/shard_map/sthi,sthj->shij/dot_general | solution.py:74
  10.8 0.2 compare_select_fusion.7
  11.3 0.8 convert_multiply_fusion
  12.2 22.3 %all_gather.17 = f32[8,2,128]{2,1,0:T(2,128)S(1)} all-gather(f32[1,2,128]{2,1,0:T(2,128)S(1)} %bitcast.206), channel_id=1, replica_groups=mesh['groups'=2,'outer'=2,'inner'=4,'head'=2] {'outer','inner'}, dimensions={0}, use_global_device_ids=true | all-gather | bytes 9216 | tf_op jit(solution)/shard_map/all_gather | solution.py:16
  34.6 1.2 %fusion.74 = (f32[2,384]{1,0:T(2,128)S(1)}, f32[2,384,384]{1,2,0:T(8,128)S(1)}) fusion(pred[384,384]{0,1:T(8,128)(4,1)S(1)} %iota_compare_fusion, f32[384,256]{1,0:T(8,128)S(1)} %copy-done.1, f32[384,256]{1,0:T(8,128)S(1)} %copy-done.2), kind=kOutput, calls=%fused_computation.96 | convolution fusion | flops 453868800 | bytes 2116608 | tf_op jit(solution)/shard_map/sthd,suhd->shtu/dot_general | solution.py:100
  36.0 2.2 %multiply_reduce_fusion = (f32[2,384]{1,0:T(2,128)S(1)}, f32[2,384,384]{1,2,0:T(8,128)}) fusion(f32[2,384]{1,0:T(2,128)S(1)} %fusion.12, f32[2,384,384]{1,2,0:T(8,128)S(1)} %get-tuple-element.159, f32[2,384]{1,0:T(2,128)S(1)} %get-tuple-element.158, f32[48,2,8,128]{3,2,1,0:T(8,128)S(1)} %copy-done.3, f32[384,256]{1,0:T(8,128)S(1)} %copy-done), kind=kOutput, calls=%fused_computation.24 | convolution fusion | flops 454163712 | bytes 3154944 | tf_op jit(solution)/shard_map/sthd,suhd->shtu/dot_general | solution.py:104
  38.3 15.6 %all-gather.5.cloned.1.call-done = f32[16,128,128]{2,1,0:T(8,128)} async-done(((f32[2,128,128]{2,1,0:T(8,128)}), f32[16,128,128]{2,1,0:T(8,128)}) %all-gather.5.cloned.1.call-update) | async-done | bytes 1048592 | tf_op jit(solution)/shard_map/all_gather | solution.py:16
  54.0 0.6 fusion.55
  54.7 2.6 %fusion.51 = f32[2,128,128]{2,1,0:T(8,128)} fusion(f32[48,2,8,128]{3,2,1,0:T(8,128)} %get-tuple-element.157, f32[384,2]{0,1:T(2,128)S(1)} %fusion.58, f32[384,256]{1,0:T(8,128)S(1)} %copy-done.2), kind=kOutput, calls=%fused_computation.76 | convolution fusion | flops 151486464 | bytes 920576 | tf_op jit(solution)/shard_map/sthi,sthj->shij/dot_general | solution.py:89
  57.3 3.4 %fusion.29 = f32[2,128,384]{2,1,0:T(8,128)} fusion(f32[48,2,8,128]{3,2,1,0:T(8,128)} %get-tuple-element.157, f32[2,384,384]{1,2,0:T(8,128)S(1)} %get-tuple-element.159, f32[2,384]{1,0:T(2,128)S(1)} %fusion.12, f32[2,384]{1,0:T(2,128)S(1)} %get-tuple-element.158), kind=kOutput, calls=%fused_computation.54 | convolution fusion | flops 453574656 | bytes 1972224 | tf_op jit(solution)/shard_map/shtu,sthd->suhd/dot_general | solution.py:109
  60.7 2.3 %convolution_bitcast_fusion.1 = f32[1,384,2,128]{1,3,2,0:T(8,128)} fusion(f32[2,384,384]{1,2,0:T(8,128)S(1)} %copy-done.8, f32[2,384]{1,0:T(2,128)S(1)} %get-tuple-element.160, f32[2,384,384]{1,2,0:T(8,128)S(1)} %get-tuple-element.159, f32[2,384]{1,0:T(2,128)S(1)} %fusion.12, f32[2,384]{1,0:T(2,128)S(1)} %get-tuple-element.158, f32[384,256]{1,0:T(8,128)S(1)} %copy-done.2), kind=kOutput, calls=%fused_computation.11 | convolution fusion | flops 454459392 | bytes 3154944 | tf_op jit(solution)/shard_map/shtu,sthd->suhd/dot_general | solution.py:108
  63.1 2.2 %convolution_bitcast_fusion.4 = f32[1,384,2,128]{1,3,2,0:T(8,128)} fusion(f32[2,384,384]{1,2,0:T(8,128)S(1)} %copy-done.8, f32[2,384]{1,0:T(2,128)S(1)} %get-tuple-element.160, f32[2,384,384]{1,2,0:T(8,128)S(1)} %get-tuple-element.159, f32[2,384]{1,0:T(2,128)S(1)} %fusion.12, f32[2,384]{1,0:T(2,128)S(1)} %get-tuple-element.158, f32[384,256]{1,0:T(8,128)S(1)} %copy-done.1), kind=kOutput, calls=%fused_computation.14 | convolution fusion | flops 454459392 | bytes 3154944 | tf_op jit(solution)/shard_map/shtu,suhd->sthd/dot_general | solution.py:107
  65.2 0.8 fusion.10
  66.2 0.5 mul.105
  66.6 0.3 fusion.19
  67.2 1.7 %fusion.3 = f32[1,384,2,128]{1,3,2,0:T(8,128)S(1)} fusion(f32[1,384,2,128]{1,3,2,0:T(8,128)} %convolution_bitcast_fusion.4, f32[1,384,2,128]{1,3,2,0:T(8,128)S(1)} %bitcast.203, f32[2,128,128]{2,1,0:T(8,128)S(1)} %get-tuple-element.118, f32[2,128]{1,0:T(2,128)S(1)} %get-tuple-element.119, f32[384,2]{0,1:T(2,128)S(1)} %fusion.57, ...), kind=kOutput, calls=%fused_computation.18 | convolution fusion | flops 151486464 | bytes 1711104 | tf_op jit(solution)/shard_map/sthj,shij->sthi/dot_general | solution.py:86
  68.9 0.9 copy.64
  69.8 25.3 %all_gather.19 = f32[8,2,128]{2,1,0:T(2,128)S(1)} all-gather(f32[1,2,128]{2,1,0:T(2,128)S(1)} %bitcast.207), channel_id=1, replica_groups=mesh['groups'=2,'outer'=2,'inner'=4,'head'=2] {'outer','inner'}, dimensions={0}, use_global_device_ids=true | all-gather | bytes 9216 | tf_op jit(solution)/shard_map/all_gather | solution.py:16
  95.1 8.1 %all-gather.7.cloned.1.call-done = f32[16,128,128]{2,1,0:T(8,128)} async-done(((f32[2,128,128]{2,1,0:T(8,128)}), f32[16,128,128]{2,1,0:T(8,128)}) %all-gather.7.cloned.1.call-update) | async-done | bytes 1048592 | tf_op jit(solution)/shard_map/all_gather | solution.py:16
  103.3 6.9 %while.27 = (s32[]{:T(128)}, f32[2,128,128]{2,1,0:T(8,128)S(1)}, f32[2,128]{1,0:T(2,128)S(1)}, s32[]{:T(128)}, f32[8,2,128,128]{3,2,1,0:T(8,128)}, /*index=5*/f3...) while((s32[]{:T(128)}, f32[2,128,128]{2,1,0:T(8,128)S(1)}, f32[2,128]{1,0:T(2,128)S(1)}, ...), condition=%wide.region_9.10_spmd, body=%wide.region_8.9_spmd.sunk | while | flops 33030 | bytes 396451 | solution.py:25
  103.3 0.9 bitcast_add_fusion.10
  104.3 0.9 bitcast_add_fusion.10
  105.3 0.9 bitcast_add_fusion.10
  106.2 0.9 bitcast_add_fusion.10
  107.2 0.9 bitcast_add_fusion.10
  108.2 0.9 bitcast_add_fusion.10
  109.2 0.9 bitcast_add_fusion.10
  110.2 0.8 convolution_add_fusion
  110.9 0.9 copy.66
  111.9 0.6 fusion.7
  112.5 0.9 copy.65
  (41 shorter events, 1.4 us)
Async XLA Ops:
  7.2 1.0 copy-start
  7.2 3.6 %copy-start.1 = (f32[384,256]{1,0:T(8,128)S(1)}, f32[384,256]{1,0:T(8,128)}, u32[]{:S(2)}) copy-start(f32[384,256]{1,0:T(8,128)} %param.9) | copy-start | bytes 1179652
  7.2 4.1 %copy-start.7 = (bf16[384,256]{1,0:T(8,128)(2,1)S(1)}, bf16[384,256]{1,0:T(8,128)(2,1)}, u32[]{:S(2)}) copy-start(bf16[384,256]{1,0:T(8,128)(2,1)} %param.11) | copy-start | bytes 589828
  7.2 46.6 %all-gather.5.cloned.1.call-start = ((), (), s32[]{:S(2)}) async-start(), calls=%async_computation | async-start | bytes 1179648 | tf_op jit(solution)/shard_map/all_gather | solution.py:16
  10.8 92.5 %all-gather.7.cloned.1.call-start = ((), (), s32[]{:S(2)}) async-start(), calls=%async_computation.1 | async-start | bytes 1179648 | tf_op jit(solution)/shard_map/all_gather | solution.py:16
  11.1 23.5 %copy-start.2 = (f32[384,256]{1,0:T(8,128)S(1)}, f32[384,256]{1,0:T(8,128)}, u32[]{:S(2)}) copy-start(f32[384,256]{1,0:T(8,128)} %param.8) | copy-start | bytes 1179652
  34.6 1.4 %copy-start.3 = (f32[48,2,8,128]{3,2,1,0:T(8,128)S(1)}, f32[48,2,8,128]{3,2,1,0:T(8,128)}, u32[]{:S(2)}) copy-start(f32[48,2,8,128]{3,2,1,0:T(8,128)} %get-tuple-element.157) | copy-start | bytes 1179652
  57.3 3.4 %copy-start.8 = (f32[2,384,384]{1,2,0:T(8,128)S(1)}, f32[2,384,384]{1,2,0:T(8,128)}, u32[]{:S(2)}) copy-start(f32[2,384,384]{1,2,0:T(8,128)} %get-tuple-element.161) | copy-start | bytes 3538948
  66.2 1.0 copy-start.4
  95.1 15.0 %copy-start.6 = (f32[2,128,384]{2,1,0:T(8,128)S(1)}, f32[2,128,384]{2,1,0:T(8,128)}, u32[]{:S(2)}) copy-start(f32[2,128,384]{2,1,0:T(8,128)} %fusion.29) | copy-start | bytes 1179652
  110.1 1.7 %copy-start.5 = (f32[1,384,2,128]{1,3,2,0:T(8,128)S(1)}, f32[1,384,2,128]{1,3,2,0:T(8,128)}, u32[]{:S(2)}) copy-start(f32[1,384,2,128]{1,3,2,0:T(8,128)} %convolution_bitcast_fusion.1) | copy-start | bytes 1179652
Sparse Core Ops, SparseCore 0:
  10.9 42.9 all-gather.4
  57.5 45.7 all-gather.6
where the time goes:
time: 121 us; the launch traced here: 120 us
  blocking collectives  47.6 us (39%)
  waiting for transfers between devices  23.7 us (20%)
  matrix products  21 us (17%)
  between operations  14.3 us (12%)
  other arithmetic  8.22 us (7%)
  local copies, waits for them, and re-layouts  4.92 us (4%)
    all_gather x2, blocking collectives, prefix(): gathered = jax.tree.map(lambda a: lax.all_gather(a, axis), part)  47.6 us
    all_gather x2, waiting for transfers between devices, prefix(): gathered = jax.tree.map(lambda a: lax.all_gather(a, axis), part)  23.7 us
    add x14, other arithmetic, add_pair(): return (earlier[0] + later[0], earlier[1] + later[1])  6.69 us
    unnamed x21, local copies, waits for them, and re-layouts  3.8 us
    dot_general x1, matrix products, shards(): jnp.einsum('shtu,sthd->suhd', probs, halfgrad, precision=highest)  3.38 us
    dot_general x1, matrix products, shards(): jnp.einsum('sthi,sthj->shij', feat_query, grad_numer, precision=highest)  2.63 us
    dot_general x1, matrix products, shards(): jnp.einsum('sthi,sthj->shij', feat_key, values, precision=highest)  2.57 us
  transfers between devices with their start and end apart: 2, of which 2 were waited for; matrix products, arithmetic and copies ran while one was open for 14% of the time, Pallas kernels for 0%

commit v1 on v0

v1 whole, which is shorter than its diff:
```python
import functools
import math

import jax
import jax.numpy as jnp
from jax import lax
from jax.experimental import pallas as pl
from jax.experimental.pallas import tpu as pltpu
from jax.sharding import PartitionSpec as P

HD = 128
SEG = 384
BLK = 128
CHUNKS = 4
MESH = pl.DeviceIdType.MESH
F32 = jnp.float32


def dot(a, b, ca, cb):
    return lax.dot_general(
        a, b, (((ca,), (cb,)), ((), ())), precision=lax.Precision.HIGHEST, preferred_element_type=F32
    )


def feature(x):
    return jnp.where(x > 0, x + 1.0, jnp.exp(jnp.minimum(x, 0.0)))


class Chain:
    def __init__(self, reverse, n_o, n_i, refs):
        (self.own, self.acc, self.xin, self.y, self.fin, self.fout, self.bin, self.bout, self.sems) = refs
        o, i = lax.axis_index("outer"), lax.axis_index("inner")
        self.n_o, self.n_i = n_o, n_i
        self.o = n_o - 1 - o if reverse else o
        self.i = n_i - 1 - i if reverse else i
        self.b = n_i - 1 - self.i
        step = -1 if reverse else 1
        self.o_next = o + step
        self.i_next = i + step
        self.i_prev = i - step
        self.steps = CHUNKS + n_o - 1 + n_i - 1

    def copy(self, src, dst, kind, c, where):
        return pltpu.make_async_remote_copy(
            src_ref=src.at[c],
            dst_ref=dst.at[c],
            send_sem=self.sems.at[2 * kind, c],
            recv_sem=self.sems.at[2 * kind + 1, c],
            device_id=where,
            device_id_type=MESH,
        )

    def x_copy(self, c):
        return self.copy(self.y, self.xin, 0, c, {"outer": self.o_next})

    def f_copy(self, c):
        return self.copy(self.fout, self.fin, 1, c, {"inner": self.i_next})

    def b_copy(self, c):
        return self.copy(self.bout, self.bin, 2, c, {"inner": self.i_prev})

    def step(self, s):
        self.x_step(s - self.o)
        self.f_step(s - self.o - self.i)
        self.b_step(s - self.o - self.b)

    def x_step(self, c):
        @pl.when((c >= 0) & (c < CHUNKS))
        def _():
            @pl.when(self.o > 0)
            def _():
                self.x_copy(c).wait_recv()
                got = self.xin[c]
                self.acc[c] = got
                self.y[c] = got + self.own[c]

            @pl.when(self.o == 0)
            def _():
                self.acc[c] = jnp.zeros_like(self.acc[c])
                self.y[c] = self.own[c]

            @pl.when(self.o < self.n_o - 1)
            def _():
                self.x_copy(c).start()

    def f_step(self, c):
        @pl.when((c >= 0) & (c < CHUNKS))
        def _():
            @pl.when(self.i > 0)
            def _():
                self.f_copy(c).wait_recv()
                got = self.fin[c]
                self.acc[c] += got
                self.fout[c] = got + self.y[c]

            @pl.when(self.i == 0)
            def _():
                self.fout[c] = self.y[c]

            @pl.when(self.i < self.n_i - 1)
            def _():
                self.f_copy(c).start()

    def b_step(self, c):
        @pl.when((c >= 0) & (c < CHUNKS) & (self.o > 0))
        def _():
            @pl.when(self.b > 0)
            def _():
                self.b_copy(c).wait_recv()
                got = self.bin[c]
                self.acc[c] += got
                self.bout[c] = got + self.xin[c]

            @pl.when(self.b == 0)
            def _():
                self.bout[c] = self.xin[c]

            @pl.when(self.b < self.n_i - 1)
            def _():
                self.b_copy(c).start()

    def finish(self):
        def one(c, _):
            @pl.when(self.o < self.n_o - 1)
            def _():
                self.x_copy(c).wait_send()

            @pl.when(self.i < self.n_i - 1)
            def _():
                self.f_copy(c).wait_send()

            @pl.when((self.o > 0) & (self.b < self.n_i - 1))
            def _():
                self.b_copy(c).wait_send()

            return 0

        lax.fori_loop(0, CHUNKS, one, 0)


def kernel(n_o, n_i, heads, q_ref, k_ref, v_ref, ct_ref, gq_ref, gk_ref, gv_ref,
           fq_ref, fk_ref, dn_ref, zb, wb, zsem, wsem, *chain_refs):
    n = n_o * n_i
    o, i = lax.axis_index("outer"), lax.axis_index("inner")
    me = o * n_i + i
    barrier = pltpu.get_barrier_semaphore()

    def peer(d):
        p = lax.rem(me + d, n)
        return p, {"outer": p // n_i, "inner": lax.rem(p, n_i)}

    def greet(d, _):
        pl.semaphore_signal(barrier, inc=1, device_id=peer(d)[1], device_id_type=MESH)
        return 0

    lax.fori_loop(1, n, greet, 0)

    def spread_copy(buf, sem, slot, where):
        return pltpu.make_async_remote_copy(
            src_ref=buf.at[slot], dst_ref=buf.at[slot],
            send_sem=sem.at[0, slot], recv_sem=sem.at[1, slot],
            device_id=where, device_id_type=MESH,
        )

    def spread_start(buf, sem):
        def one(d, _):
            p, where = peer(d)
            pltpu.make_async_remote_copy(
                src_ref=buf.at[me], dst_ref=buf.at[me],
                send_sem=sem.at[0, p], recv_sem=sem.at[1, me],
                device_id=where, device_id_type=MESH,
            ).start()
            return 0

        lax.fori_loop(1, n, one, 0)

    def spread_wait(buf, sem):
        def one(d, _):
            p, where = peer(d)
            spread_copy(buf, sem, p, where).wait_recv()
            return 0

        lax.fori_loop(1, n, one, 0)

    def spread_finish(buf, sem):
        def one(d, _):
            p, where = peer(d)
            spread_copy(buf, sem, p, where).wait_send()
            return 0

        lax.fori_loop(1, n, one, 0)

    before = Chain(False, n_o, n_i, chain_refs[:9])
    after = Chain(True, n_o, n_i, chain_refs[9:])
    per = CHUNKS // heads
    rows = HD // per
    cols = [slice(h * HD, (h + 1) * HD) for h in range(heads)]

    def put(ref, h, value):
        for c in range(per):
            ref[h * per + c] = value[c * rows:(c + 1) * rows]

    def get(ref, h):
        return jnp.concatenate([ref[h * per + c] for c in range(per)], axis=0)

    sums = []
    for h in range(heads):
        fk = feature(k_ref[:, cols[h]])
        fk_ref[:, cols[h]] = fk
        sums.append(jnp.sum(fk, axis=0, keepdims=True))
    zb[me] = jnp.concatenate(sums, axis=0)
    pl.semaphore_wait(barrier, n - 1)
    spread_start(zb, zsem)
    for h in range(heads):
        put(before.own, h, dot(fk_ref[:, cols[h]], v_ref[:, cols[h]], 0, 0))
    before.step(0)

    for h in range(heads):
        fq_ref[:, cols[h]] = feature(q_ref[:, cols[h]])
    spread_wait(zb, zsem)
    slots = lax.broadcasted_iota(jnp.int32, (n, heads, HD), 0)
    znorm = jnp.sum(jnp.where(slots < me, zb[...], 0.0), axis=0)
    dens, raws = [], []
    for h in range(heads):
        fq = fq_ref[:, cols[h]]
        raw = jnp.sum(fq * znorm[h:h + 1], axis=1, keepdims=True)
        den = jnp.maximum(raw, 1.0)
        dn = (0.5 * ct_ref[:, cols[h]].astype(F32)) / den
        dn_ref[:, cols[h]] = dn
        raws.append(raw)
        dens.append(den)
        put(after.own, h, dot(fq, dn, 0, 0))

    scale = 1.0 / math.sqrt(HD)
    last = SEG // BLK - 1

    def attend(h, b):
        t, u = slice(b * BLK, (b + 1) * BLK), slice(0, (b + 1) * BLK)
        q, g = q_ref[t, cols[h]], 0.5 * ct_ref[t, cols[h]].astype(F32)
        k, v = k_ref[u, cols[h]], v_ref[u, cols[h]]
        s = dot(k, q, 1, 1) * scale
        size = (b + 1) * BLK
        row = lax.broadcasted_iota(jnp.int32, (size, BLK), 0)
        col = lax.broadcasted_iota(jnp.int32, (size, BLK), 1) + b * BLK
        s = jnp.where(row <= col, s, -jnp.inf)
        e = jnp.exp(s - jnp.max(s, axis=0, keepdims=True))
        p = e / jnp.sum(e, axis=0, keepdims=True)
        dp = dot(v, g, 1, 1)
        ds = p * (dp - jnp.sum(dp * p, axis=0, keepdims=True)) * scale
        gk, gv = dot(ds, q, 1, 0), dot(p, g, 1, 0)
        if b == last:
            gk_ref[u, cols[h]] = gk
            gv_ref[u, cols[h]] = gv
        else:
            gk_ref[u, cols[h]] += gk
            gv_ref[u, cols[h]] += gv
        gq_ref[t, cols[h]] = dot(ds, k, 0, 0)

    pieces = [(h, b) for h in range(heads) for b in range(last, -1, -1)]
    for s in range(1, before.steps + 1):
        if s < before.steps:
            before.step(s)
        after.step(s - 1)
        if pieces:
            attend(*pieces.pop(0))
    while pieces:
        attend(*pieces.pop(0))

    extra = []
    for h in range(heads):
        memory = get(before.acc, h)
        fq, dn = fq_ref[:, cols[h]], dn_ref[:, cols[h]]
        numer = dot(fq, memory, 1, 0)
        dden = jnp.where(raws[h] > 1.0, -jnp.sum(dn * numer, axis=1, keepdims=True) / dens[h], 0.0)
        extra.append(jnp.sum(fq * dden, axis=0, keepdims=True))
        grad = dot(dn, memory, 1, 1) + dden * znorm[h:h + 1]
        gq_ref[:, cols[h]] += grad * jnp.minimum(fq, 1.0)
    wb[me] = jnp.concatenate(extra, axis=0)
    spread_start(wb, wsem)
    later = []
    for h in range(heads):
        memory = get(after.acc, h)
        gv_ref[:, cols[h]] += dot(fk_ref[:, cols[h]], memory, 1, 0)
        later.append(dot(v_ref[:, cols[h]], memory, 1, 1))
    spread_wait(wb, wsem)
    lz = jnp.sum(jnp.where(slots > me, wb[...], 0.0), axis=0)
    for h in range(heads):
        gk_ref[:, cols[h]] += (later[h] + lz[h:h + 1]) * jnp.minimum(fk_ref[:, cols[h]], 1.0)
    before.finish()
    after.finish()
    spread_finish(zb, zsem)
    spread_finish(wb, wsem)


def shards(n_o, n_i, queries, key_states, value_states, cotangent):
    rows, columns = queries.shape
    assert rows == SEG
    heads = columns // HD
    n = n_o * n_i
    unit = pltpu.VMEM((CHUNKS, heads * HD // CHUNKS, HD), F32)
    chain = [unit] * 8 + [pltpu.SemaphoreType.DMA((6, CHUNKS))]
    full = pltpu.VMEM((rows, columns), F32)
    small = pltpu.VMEM((n, heads, HD), F32)
    vmem = pl.BlockSpec(memory_space=pltpu.VMEM)
    return tuple(pl.pallas_call(
        functools.partial(kernel, n_o, n_i, heads),
        out_shape=[jax.ShapeDtypeStruct((rows, columns), F32)] * 3,
        in_specs=[vmem] * 4,
        out_specs=[vmem] * 3,
        scratch_shapes=[full, full, full, small, small,
                        pltpu.SemaphoreType.DMA((2, n)), pltpu.SemaphoreType.DMA((2, n))] + chain + chain,
        compiler_params=pltpu.CompilerParams(
            collective_id=0, has_side_effects=True, vmem_limit_bytes=48 * 1024 * 1024
        ),
    )(queries, key_states, value_states, cotangent))


def solution(mesh):
    spec = P(("groups", "outer", "inner"), "head")
    body = functools.partial(shards, mesh.shape["outer"], mesh.shape["inner"])
    return jax.shard_map(body, mesh=mesh, in_specs=(spec,) * 4, out_specs=(spec,) * 3, check_vma=False)
```

time: 121 us -> 45 us (0.37)
  blocking collectives: 47.6 us -> 0 us
  Pallas kernels: 0 us -> 37.9 us
  waiting for transfers between devices: 23.7 us -> 0 us
  matrix products: 21 us -> 0 us
  between operations: 14.3 us -> 0.65 us
  other arithmetic: 8.22 us -> 0 us
  local copies, waits for them, and re-layouts: 4.92 us -> 6.14 us
    all_gather x2 -> x0, blocking collectives: 47.6 us -> none  [prefix(): gathered = jax.tree.map(lambda a: lax.all_gather(a, axis), part)]
    pallas_call x0 -> x1, Pallas kernels: none -> 37.9 us  [shards(): pl.pallas_call(functools.partial(kernel, n_o, n_i, heads), out_shape=[jax...]
    all_gather x2 -> x0, waiting for transfers between devices: 23.7 us -> none  [prefix(): gathered = jax.tree.map(lambda a: lax.all_gather(a, axis), part)]
    dot_general x12 -> x0, matrix products: 21 us -> none  [the longest x1 3.38 us: shards(): jnp.einsum('shtu,sthd->suhd', probs, halfgrad, precision=highest)]
    add x14 -> x0, other arithmetic: 6.69 us -> none  [add_pair(): return (earlier[0] + later[0], earlier[1] + later[1])]
    unnamed x21 -> x11, local copies, waits for them, and re-layouts: 3.8 us -> 6.14 us
  transfers between devices with their start and end apart: 2 -> 0, of which waited for: 2 -> 0; matrix products, arithmetic and copies ran while one was open for 14% -> 0% of each run, Pallas kernels for 0% -> 0%
where the time goes in v1:
time: 45 us; the launch traced here: 44.7 us
  Pallas kernels  37.9 us (84%)
  local copies, waits for them, and re-layouts  6.14 us (14%)
  between operations  0.65 us (1%)
    pallas_call x1, Pallas kernels, shards(): pl.pallas_call(functools.partial(kernel, n_o, n_i, heads), out_shape=[jax...  37.9 us
    unnamed x11, local copies, waits for them, and re-layouts  6.14 us

profile of v1, /device:TPU:0, one launch (start us, length us, event | category | flops | bytes accessed | tf_op | source)
XLA Modules:
  0.0 44.7 jit_solution(10237609233368992854)
XLA Ops:
  0.6 0.0 copy-start
  0.6 1.0 %copy-done = f32[384,256]{1,0:T(8,128)S(1)} copy-done((f32[384,256]{1,0:T(8,128)S(1)}, f32[384,256]{1,0:T(8,128)}, u32[]{:S(2)}) %copy-start) | copy-done | bytes 393240
  1.6 0.0 copy-start.1
  1.6 1.0 %copy-done.1 = f32[384,256]{1,0:T(8,128)S(1)} copy-done((f32[384,256]{1,0:T(8,128)S(1)}, f32[384,256]{1,0:T(8,128)}, u32[]{:S(2)}) %copy-start.1) | copy-done | bytes 393240
  2.6 0.0 copy-start.2
  2.6 1.0 %copy-done.2 = f32[384,256]{1,0:T(8,128)S(1)} copy-done((f32[384,256]{1,0:T(8,128)S(1)}, f32[384,256]{1,0:T(8,128)}, u32[]{:S(2)}) %copy-start.2) | copy-done | bytes 393240
  3.6 0.0 copy-start.3
  3.6 0.9 %copy-done.3 = bf16[384,256]{1,0:T(8,128)(2,1)S(1)} copy-done((bf16[384,256]{1,0:T(8,128)(2,1)S(1)}, bf16[384,256]{1,0:T(8,128)(2,1)}, u32[]{:S(2)}) %copy-start.3) | copy-done | bytes 196632
  4.5 37.9 %shard_map.67 = (f32[384,256]{1,0:T(8,128)S(1)}, f32[384,256]{1,0:T(8,128)S(1)}, f32[384,256]{1,0:T(8,128)S(1)}) custom-call(f32[384,256]{1,0:T(8,128)S(1)} %copy-done, f32[384,256]{1,0:T(8,128)S(1)} %copy-done.1, f32[384,256]{1,0:T(8,128)S(1)} %copy-done.2, bf16[384,256]{1,0:T(8,128)(2,1)S(1)} %copy-done.3), custom_call_target="tpu_custom_call" | custom-call | tf_op jit(solution)/shard_map/pallas_call | solution.py:305
  42.5 0.7 %copy.10 = f32[384,256]{1,0:T(8,128)} copy(f32[384,256]{1,0:T(8,128)S(1)} %get-tuple-element.6) | data formatting | bytes 786432
  43.2 0.7 %copy.11 = f32[384,256]{1,0:T(8,128)} copy(f32[384,256]{1,0:T(8,128)S(1)} %get-tuple-element.7) | data formatting | bytes 786432
  44.0 0.7 %copy.12 = f32[384,256]{1,0:T(8,128)} copy(f32[384,256]{1,0:T(8,128)S(1)} %get-tuple-element.8) | data formatting | bytes 786432
Async XLA Ops:
  0.6 1.0 %copy-start = (f32[384,256]{1,0:T(8,128)S(1)}, f32[384,256]{1,0:T(8,128)}, u32[]{:S(2)}) copy-start(f32[384,256]{1,0:T(8,128)} %q_ref.1) | copy-start | bytes 1179652
  1.6 1.0 %copy-start.1 = (f32[384,256]{1,0:T(8,128)S(1)}, f32[384,256]{1,0:T(8,128)}, u32[]{:S(2)}) copy-start(f32[384,256]{1,0:T(8,128)} %k_ref.1) | copy-start | bytes 1179652
  2.6 1.0 %copy-start.2 = (f32[384,256]{1,0:T(8,128)S(1)}, f32[384,256]{1,0:T(8,128)}, u32[]{:S(2)}) copy-start(f32[384,256]{1,0:T(8,128)} %v_ref.1) | copy-start | bytes 1179652
  3.6 0.9 %copy-start.3 = (bf16[384,256]{1,0:T(8,128)(2,1)S(1)}, bf16[384,256]{1,0:T(8,128)(2,1)}, u32[]{:S(2)}) copy-start(bf16[384,256]{1,0:T(8,128)(2,1)} %ct_ref.1) | copy-start | bytes 589828

commit v2 on v1

v2 whole, which is shorter than its diff:
```python
import functools
import math

import jax
import jax.numpy as jnp
from jax import lax
from jax.experimental import pallas as pl
from jax.experimental.pallas import tpu as pltpu
from jax.sharding import PartitionSpec as P

HD = 128
SEG = 384
BLK = 128
FILL = (1, 1, 1, 1)
MESH = pl.DeviceIdType.MESH
F32 = jnp.float32


def dot(a, b, ca, cb):
    return lax.dot_general(
        a, b, (((ca,), (cb,)), ((), ())), precision=lax.Precision.HIGHEST, preferred_element_type=F32
    )


def feature(x):
    return jnp.where(x > 0, x + 1.0, jnp.exp(jnp.minimum(x, 0.0)))


def kernel(n_o, n_i, heads, q_hbm, k_hbm, v_hbm, ct_hbm, gq_ref, gk_ref, gv_ref,
           q_ref, k_ref, v_ref, ct_ref, fq_ref, fk_ref, dn_ref, zb, wb,
           p_out, p_in, e_out, e_in, a_out, a_in, f_out, f_in, load_sem, sems):
    n = n_o * n_i
    me = lax.axis_index("outer") * n_i + lax.axis_index("inner")
    barrier = pltpu.get_barrier_semaphore()
    loads = [
        pltpu.make_async_copy(src, dst, load_sem.at[j])
        for j, (src, dst) in enumerate(((k_hbm, k_ref), (v_hbm, v_ref), (q_hbm, q_ref), (ct_hbm, ct_ref)))
    ]
    for load in loads:
        load.start()

    def peers(body):
        def one(d, _):
            p = lax.rem(me + d, n)
            body(p, {"outer": p // n_i, "inner": lax.rem(p, n_i)})
            return 0

        lax.fori_loop(1, n, one, 0)

    class Exchange:
        def __init__(self, kind, src, dst):
            self.kind, self.src, self.dst = kind, src, dst

        def copy(self, p, where, slot):
            return pltpu.make_async_remote_copy(
                src_ref=self.dst.at[me] if self.src is None else self.src.at[p],
                dst_ref=self.dst.at[slot],
                send_sem=sems.at[2 * self.kind, p],
                recv_sem=sems.at[2 * self.kind + 1, slot],
                device_id=where,
                device_id_type=MESH,
            )

        def start(self):
            peers(lambda p, where: self.copy(p, where, me).start())
            if self.src is not None:
                self.dst[me] = self.src[me]

        def wait(self):
            peers(lambda p, where: self.copy(p, where, p).wait_recv())

        def finish(self):
            peers(lambda p, where: self.copy(p, where, p).wait_send())

    z_ex, w_ex = Exchange(0, None, zb), Exchange(1, None, wb)
    p_ex, e_ex = Exchange(2, p_out, p_in), Exchange(3, e_out, e_in)
    a_ex, f_ex = Exchange(4, a_out, a_in), Exchange(5, f_out, f_in)

    peers(lambda p, where: pl.semaphore_signal(barrier, inc=1, device_id=where, device_id_type=MESH))

    per = n // heads
    rows = HD // per
    cols = [slice(h * HD, (h + 1) * HD) for h in range(heads)]

    def put(ref, h, value):
        for c in range(per):
            ref[h * per + c] = value[c * rows:(c + 1) * rows]

    def get(ref, h):
        return jnp.concatenate([ref[h * per + c] for c in range(per)], axis=0)

    sums = []
    loads[0].wait()
    for h in range(heads):
        fk = feature(k_ref[:, cols[h]])
        fk_ref[:, cols[h]] = fk
        sums.append(jnp.sum(fk, axis=0, keepdims=True))
    zb[me] = jnp.concatenate(sums, axis=0)
    loads[1].wait()
    for h in range(heads):
        put(p_out, h, dot(fk_ref[:, cols[h]], v_ref[:, cols[h]], 0, 0))
    loads[2].wait()
    for h in range(heads):
        fq_ref[:, cols[h]] = feature(q_ref[:, cols[h]])
    loads[3].wait()
    pl.semaphore_wait(barrier, n - 1)
    z_ex.start()
    p_ex.start()

    scale = 1.0 / math.sqrt(HD)
    last = SEG // BLK - 1

    def attend(h, b):
        t, u = slice(b * BLK, (b + 1) * BLK), slice(0, (b + 1) * BLK)
        q, g = q_ref[t, cols[h]], 0.5 * ct_ref[t, cols[h]].astype(F32)
        k, v = k_ref[u, cols[h]], v_ref[u, cols[h]]
        s = dot(k, q, 1, 1) * scale
        size = (b + 1) * BLK
        row = lax.broadcasted_iota(jnp.int32, (size, BLK), 0)
        col = lax.broadcasted_iota(jnp.int32, (size, BLK), 1) + b * BLK
        s = jnp.where(row <= col, s, -jnp.inf)
        e = jnp.exp(s - jnp.max(s, axis=0, keepdims=True))
        p = e / jnp.sum(e, axis=0, keepdims=True)
        dp = dot(v, g, 1, 1)
        ds = p * (dp - jnp.sum(dp * p, axis=0, keepdims=True)) * scale
        gk, gv = dot(ds, q, 1, 0), dot(p, g, 1, 0)
        if b == last:
            gk_ref[u, cols[h]] = gk
            gv_ref[u, cols[h]] = gv
        else:
            gk_ref[u, cols[h]] += gk
            gv_ref[u, cols[h]] += gv
        gq_ref[t, cols[h]] = dot(ds, k, 0, 0)

    pieces = [(h, b) for h in range(heads) for b in range(last, -1, -1)]

    def fill(count):
        for _ in range(count):
            attend(*pieces.pop(0))

    fill(FILL[0])
    z_ex.wait()
    slots = lax.broadcasted_iota(jnp.int32, (n, heads, HD), 0)
    znorm = jnp.sum(jnp.where(slots < me, zb[...], 0.0), axis=0)
    dens, raws = [], []
    for h in range(heads):
        fq = fq_ref[:, cols[h]]
        raw = jnp.sum(fq * znorm[h:h + 1], axis=1, keepdims=True)
        den = jnp.maximum(raw, 1.0)
        dn = (0.5 * ct_ref[:, cols[h]].astype(F32)) / den
        dn_ref[:, cols[h]] = dn
        raws.append(raw)
        dens.append(den)
        put(a_out, h, dot(fq, dn, 0, 0))
    a_ex.start()
    fill(FILL[1])
    p_ex.wait()
    total = jnp.zeros_like(p_in[0])
    for l in range(n):
        e_out[l] = total
        total = total + p_in[l]
    e_ex.start()
    fill(FILL[2])
    a_ex.wait()
    total = jnp.zeros_like(a_in[0])
    for l in range(n - 1, -1, -1):
        f_out[l] = total
        total = total + a_in[l]
    f_ex.start()
    fill(FILL[3])
    e_ex.wait()
    extra = []
    memories = []
    for h in range(heads):
        memory = get(e_in, h)
        memories.append(memory)
        fq = fq_ref[:, cols[h]]
        numer = dot(fq, memory, 1, 0)
        dden = jnp.where(raws[h] > 1.0, -jnp.sum(dn_ref[:, cols[h]] * numer, axis=1, keepdims=True) / dens[h], 0.0)
        dens[h] = dden
        extra.append(jnp.sum(fq * dden, axis=0, keepdims=True))
    wb[me] = jnp.concatenate(extra, axis=0)
    w_ex.start()
    fill(len(pieces))
    for h in range(heads):
        grad = dot(dn_ref[:, cols[h]], memories[h], 1, 1) + dens[h] * znorm[h:h + 1]
        gq_ref[:, cols[h]] += grad * jnp.minimum(fq_ref[:, cols[h]], 1.0)
    f_ex.wait()
    later = []
    for h in range(heads):
        memory = get(f_in, h)
        gv_ref[:, cols[h]] += dot(fk_ref[:, cols[h]], memory, 1, 0)
        later.append(dot(v_ref[:, cols[h]], memory, 1, 1))
    w_ex.wait()
    lz = jnp.sum(jnp.where(slots > me, wb[...], 0.0), axis=0)
    for h in range(heads):
        gk_ref[:, cols[h]] += (later[h] + lz[h:h + 1]) * jnp.minimum(fk_ref[:, cols[h]], 1.0)
    for ex in (z_ex, p_ex, a_ex, e_ex, f_ex, w_ex):
        ex.finish()


def shards(n_o, n_i, queries, key_states, value_states, cotangent):
    rows, columns = queries.shape
    assert rows == SEG
    heads = columns // HD
    n = n_o * n_i
    full = pltpu.VMEM((rows, columns), F32)
    small = pltpu.VMEM((n, heads, HD), F32)
    part = pltpu.VMEM((n, heads * HD // n, HD), F32)
    vmem = pl.BlockSpec(memory_space=pltpu.VMEM)
    hbm = pl.BlockSpec(memory_space=pltpu.HBM)
    return tuple(pl.pallas_call(
        functools.partial(kernel, n_o, n_i, heads),
        out_shape=[jax.ShapeDtypeStruct((rows, columns), F32)] * 3,
        in_specs=[hbm] * 4,
        out_specs=[vmem] * 3,
        scratch_shapes=[full, full, full, pltpu.VMEM((rows, columns), jnp.bfloat16), full, full, full,
                        small, small] + [part] * 8
        + [pltpu.SemaphoreType.DMA((4,)), pltpu.SemaphoreType.DMA((12, n))],
        compiler_params=pltpu.CompilerParams(
            collective_id=0, has_side_effects=True, vmem_limit_bytes=48 * 1024 * 1024
        ),
    )(queries, key_states, value_states, cotangent))


def solution(mesh):
    spec = P(("groups", "outer", "inner"), "head")
    body = functools.partial(shards, mesh.shape["outer"], mesh.shape["inner"])
    return jax.shard_map(body, mesh=mesh, in_specs=(spec,) * 4, out_specs=(spec,) * 3, check_vma=False)
```

time: 45 us -> 33 us (0.73)
  Pallas kernels: 37.9 us -> 26 us
    pallas_call x1, Pallas kernels: 37.9 us -> 26 us  [shards(): pl.pallas_call(functools.partial(kernel, n_o, n_i, heads), out_shape=[jax...]
where the time goes in v2:
time: 33 us; the launch traced here: 32.8 us
  Pallas kernels  26 us (79%)
  local copies, waits for them, and re-layouts  6.14 us (19%)
  between operations  0.65 us (2%)
    pallas_call x1, Pallas kernels, shards(): pl.pallas_call(functools.partial(kernel, n_o, n_i, heads), out_shape=[jax...  26 us
    unnamed x11, local copies, waits for them, and re-layouts  6.14 us

profile of v2, /device:TPU:0, one launch (start us, length us, event | category | flops | bytes accessed | tf_op | source)
XLA Modules:
  0.0 32.8 jit_solution(4012224773814167770)
XLA Ops:
  0.6 0.0 copy-start
  0.6 1.0 %copy-done = f32[384,256]{1,0:T(8,128)S(1)} copy-done((f32[384,256]{1,0:T(8,128)S(1)}, f32[384,256]{1,0:T(8,128)}, u32[]{:S(2)}) %copy-start) | copy-done | bytes 393240
  1.6 0.0 copy-start.1
  1.6 1.0 %copy-done.1 = f32[384,256]{1,0:T(8,128)S(1)} copy-done((f32[384,256]{1,0:T(8,128)S(1)}, f32[384,256]{1,0:T(8,128)}, u32[]{:S(2)}) %copy-start.1) | copy-done | bytes 393240
  2.6 0.0 copy-start.2
  2.6 1.0 %copy-done.2 = f32[384,256]{1,0:T(8,128)S(1)} copy-done((f32[384,256]{1,0:T(8,128)S(1)}, f32[384,256]{1,0:T(8,128)}, u32[]{:S(2)}) %copy-start.2) | copy-done | bytes 393240
  3.6 0.0 copy-start.3
  3.6 0.9 %copy-done.3 = bf16[384,256]{1,0:T(8,128)(2,1)S(1)} copy-done((bf16[384,256]{1,0:T(8,128)(2,1)S(1)}, bf16[384,256]{1,0:T(8,128)(2,1)}, u32[]{:S(2)}) %copy-start.3) | copy-done | bytes 196632
  4.5 26.0 %shard_map.67 = (f32[384,256]{1,0:T(8,128)S(1)}, f32[384,256]{1,0:T(8,128)S(1)}, f32[384,256]{1,0:T(8,128)S(1)}) custom-call(f32[384,256]{1,0:T(8,128)S(1)} %copy-done, f32[384,256]{1,0:T(8,128)S(1)} %copy-done.1, f32[384,256]{1,0:T(8,128)S(1)} %copy-done.2, bf16[384,256]{1,0:T(8,128)(2,1)S(1)} %copy-done.3), custom_call_target="tpu_custom_call" | custom-call | tf_op jit(solution)/shard_map/pallas_call | solution.py:212
  30.5 0.7 %copy.10 = f32[384,256]{1,0:T(8,128)} copy(f32[384,256]{1,0:T(8,128)S(1)} %get-tuple-element.6) | data formatting | bytes 786432
  31.3 0.7 %copy.11 = f32[384,256]{1,0:T(8,128)} copy(f32[384,256]{1,0:T(8,128)S(1)} %get-tuple-element.7) | data formatting | bytes 786432
  32.0 0.7 %copy.12 = f32[384,256]{1,0:T(8,128)} copy(f32[384,256]{1,0:T(8,128)S(1)} %get-tuple-element.8) | data formatting | bytes 786432
Async XLA Ops:
  0.6 1.0 %copy-start = (f32[384,256]{1,0:T(8,128)S(1)}, f32[384,256]{1,0:T(8,128)}, u32[]{:S(2)}) copy-start(f32[384,256]{1,0:T(8,128)} %q_hbm.1) | copy-start | bytes 1179652
  1.6 1.0 %copy-start.1 = (f32[384,256]{1,0:T(8,128)S(1)}, f32[384,256]{1,0:T(8,128)}, u32[]{:S(2)}) copy-start(f32[384,256]{1,0:T(8,128)} %k_hbm.1) | copy-start | bytes 1179652
  2.6 1.0 %copy-start.2 = (f32[384,256]{1,0:T(8,128)S(1)}, f32[384,256]{1,0:T(8,128)}, u32[]{:S(2)}) copy-start(f32[384,256]{1,0:T(8,128)} %v_hbm.1) | copy-start | bytes 1179652
  3.6 0.9 %copy-start.3 = (bf16[384,256]{1,0:T(8,128)(2,1)S(1)}, bf16[384,256]{1,0:T(8,128)(2,1)}, u32[]{:S(2)}) copy-start(bf16[384,256]{1,0:T(8,128)(2,1)} %ct_hbm.1) | copy-start | bytes 589828

commit v3 on v2

--- a/solution.py
+++ b/solution.py
@@ -26,9 +26,9 @@
     return jnp.where(x > 0, x + 1.0, jnp.exp(jnp.minimum(x, 0.0)))
 
 
-def kernel(n_o, n_i, heads, q_hbm, k_hbm, v_hbm, ct_hbm, gq_ref, gk_ref, gv_ref,
-           q_ref, k_ref, v_ref, ct_ref, fq_ref, fk_ref, dn_ref, zb, wb,
-           p_out, p_in, e_out, e_in, a_out, a_in, f_out, f_in, load_sem, sems):
+def kernel(n_o, n_i, heads, q_hbm, k_hbm, v_hbm, ct_hbm, gq_ref, gk_ref, gv_ref, fk_ref, v_ref, f_in, lz_ref,
+           q_ref, k_ref, ct_ref, fq_ref, dn_ref, zb, wb,
+           p_out, p_in, e_out, e_in, a_out, a_in, f_out, load_sem, sems):
     n = n_o * n_i
     me = lax.axis_index("outer") * n_i + lax.axis_index("inner")
     barrier = pltpu.get_barrier_semaphore()
@@ -45,7 +45,7 @@
             body(p, {"outer": p // n_i, "inner": lax.rem(p, n_i)})
             return 0
 
-        lax.fori_loop(1, n, one, 0)
+        lax.fori_loop(1, n, one, 0, unroll=n <= 8)
 
     class Exchange:
         def __init__(self, kind, src, dst):
@@ -186,17 +186,30 @@
         grad = dot(dn_ref[:, cols[h]], memories[h], 1, 1) + dens[h] * znorm[h:h + 1]
         gq_ref[:, cols[h]] += grad * jnp.minimum(fq_ref[:, cols[h]], 1.0)
     f_ex.wait()
-    later = []
-    for h in range(heads):
-        memory = get(f_in, h)
-        gv_ref[:, cols[h]] += dot(fk_ref[:, cols[h]], memory, 1, 0)
-        later.append(dot(v_ref[:, cols[h]], memory, 1, 1))
     w_ex.wait()
-    lz = jnp.sum(jnp.where(slots > me, wb[...], 0.0), axis=0)
-    for h in range(heads):
-        gk_ref[:, cols[h]] += (later[h] + lz[h:h + 1]) * jnp.minimum(fk_ref[:, cols[h]], 1.0)
+    lz_ref[...] = jnp.sum(jnp.where(slots > me, wb[...], 0.0), axis=0)
     for ex in (z_ex, p_ex, a_ex, e_ex, f_ex, w_ex):
         ex.finish()
+
+
+def closing(heads, gq_ref, gk_ref, gv_ref, fk_ref, v_ref, f_ref, lz_ref, gq_hbm, gk_hbm, gv_hbm, gk_out, gv_out, sems):
+    stores = [
+        pltpu.make_async_copy(src, dst, sems.at[j])
+        for j, (src, dst) in enumerate(((gq_ref, gq_hbm), (gv_out, gv_hbm), (gk_out, gk_hbm)))
+    ]
+    stores[0].start()
+    per = f_ref.shape[0] // heads
+    cols = [slice(h * HD, (h + 1) * HD) for h in range(heads)]
+    memories = [jnp.concatenate([f_ref[h * per + c] for c in range(per)], axis=0) for h in range(heads)]
+    for h in range(heads):
+        gv_out[:, cols[h]] = gv_ref[:, cols[h]] + dot(fk_ref[:, cols[h]], memories[h], 1, 0)
+    stores[1].start()
+    for h in range(heads):
+        later = dot(v_ref[:, cols[h]], memories[h], 1, 1) + lz_ref[h:h + 1]
+        gk_out[:, cols[h]] = gk_ref[:, cols[h]] + later * jnp.minimum(fk_ref[:, cols[h]], 1.0)
+    stores[2].start()
+    for store in stores:
+        store.wait()
 
 
 def shards(n_o, n_i, queries, key_states, value_states, cotangent):
@@ -209,18 +222,28 @@
     part = pltpu.VMEM((n, heads * HD // n, HD), F32)
     vmem = pl.BlockSpec(memory_space=pltpu.VMEM)
     hbm = pl.BlockSpec(memory_space=pltpu.HBM)
-    return tuple(pl.pallas_call(
+    array = jax.ShapeDtypeStruct((rows, columns), F32)
+    held = [array] * 5 + [jax.ShapeDtypeStruct(part.shape, F32), jax.ShapeDtypeStruct((heads, HD), F32)]
+    parts = pl.pallas_call(
         functools.partial(kernel, n_o, n_i, heads),
-        out_shape=[jax.ShapeDtypeStruct((rows, columns), F32)] * 3,
+        out_shape=held,
         in_specs=[hbm] * 4,
-        out_specs=[vmem] * 3,
-        scratch_shapes=[full, full, full, pltpu.VMEM((rows, columns), jnp.bfloat16), full, full, full,
-                        small, small] + [part] * 8
+        out_specs=[vmem] * 7,
+        scratch_shapes=[full, full, pltpu.VMEM((rows, columns), jnp.bfloat16), full, full,
+                        small, small] + [part] * 7
         + [pltpu.SemaphoreType.DMA((4,)), pltpu.SemaphoreType.DMA((12, n))],
         compiler_params=pltpu.CompilerParams(
             collective_id=0, has_side_effects=True, vmem_limit_bytes=48 * 1024 * 1024
         ),
-    )(queries, key_states, value_states, cotangent))
+    )(*(pltpu.with_memory_space_constraint(x, pltpu.HBM) for x in (queries, key_states, value_states, cotangent)))
+    return tuple(pl.pallas_call(
+        functools.partial(closing, heads),
+        out_shape=[array] * 3,
+        in_specs=[vmem] * 7,
+        out_specs=[hbm] * 3,
+        scratch_shapes=[full, full, pltpu.SemaphoreType.DMA((3,))],
+        compiler_params=pltpu.CompilerParams(vmem_limit_bytes=24 * 1024 * 1024),
+    )(*parts))
 
 
 def solution(mesh):

time: 33 us -> 26.6 us (0.81)
  local copies, waits for them, and re-layouts: 6.14 us -> 0 us
    unnamed x11 -> x0, local copies, waits for them, and re-layouts: 6.14 us -> none
    pallas_call x1 -> x2, Pallas kernels: 26 us -> 25.8 us  [the longest x1 24.2 us: shards(): pl.pallas_call(functools.partial(kernel, n_o, n_i, heads), out_shape=held...]
where the time goes in v3:
time: 26.6 us; the launch traced here: 26.4 us
  Pallas kernels  25.8 us (97%)
  between operations  0.64 us (2%)
    pallas_call x1, Pallas kernels, shards(): pl.pallas_call(functools.partial(kernel, n_o, n_i, heads), out_shape=held...  24.2 us
    pallas_call x1, Pallas kernels, shards(): pl.pallas_call(functools.partial(closing, heads), out_shape=[array] * 3,...  1.57 us

profile of v3, /device:TPU:0, one launch (start us, length us, event | category | flops | bytes accessed | tf_op | source)
XLA Modules:
  0.0 26.4 jit_solution(11553261719071674243)
XLA Ops:
  0.6 24.2 %shard_map.67 = (f32[384,256]{1,0:T(8,128)S(1)}, f32[384,256]{1,0:T(8,128)S(1)}, f32[384,256]{1,0:T(8,128)S(1)}, f32[384,256]{1,0:T(8,128)S(1)}, f32[384,256]{1,...) custom-call(f32[384,256]{1,0:T(8,128)} %q_hbm.1, f32[384,256]{1,0:T(8,128)} %k_hbm.1, f32[384,256]{1,0:T(8,128)} %v_hbm.1, ...), custom_call_target="tpu_custom_call" | custom-call | tf_op jit(solution)/shard_map/pallas_call | solution.py:227
  24.9 1.6 %shard_map.68 = (f32[384,256]{1,0:T(8,128)}, f32[384,256]{1,0:T(8,128)}, f32[384,256]{1,0:T(8,128)}) custom-call(f32[384,256]{1,0:T(8,128)S(1)} %get-tuple-element.10.gq_ref, f32[384,256]{1,0:T(8,128)S(1)} %get-tuple-element.11.gk_ref, f32[384,256]{1,0:T(8,128)S(1)} %get-tuple-element.12.gv_ref, f32[384,256]{1,0:T(8,128)S(1)} %get-tuple-element.13.fk_ref, ...), custom_call_target="tpu_custom_call" | custom-call | tf_op jit(solution)/shard_map/pallas_call | solution.py:239

commit v4 on v3

--- a/solution.py
+++ b/solution.py
@@ -11,7 +11,7 @@
 HD = 128
 SEG = 384
 BLK = 128
-FILL = (1, 1, 1, 1)
+FILL = (1, 2, 1, 1)
 MESH = pl.DeviceIdType.MESH
 F32 = jnp.float32
 
@@ -48,8 +48,17 @@
         lax.fori_loop(1, n, one, 0, unroll=n <= 8)
 
     class Exchange:
-        def __init__(self, kind, src, dst):
+        def __init__(self, kind, src, dst, idle_from=-1, idle_to=-1):
             self.kind, self.src, self.dst = kind, src, dst
+            self.idle_from, self.idle_to = idle_from, idle_to
+
+        def used(self, sender, receiver, act):
+            if self.idle_from >= 0:
+                pl.when(sender != self.idle_from)(act)
+            elif self.idle_to >= 0:
+                pl.when(receiver != self.idle_to)(act)
+            else:
+                act()
 
         def copy(self, p, where, slot):
             return pltpu.make_async_remote_copy(
@@ -62,19 +71,24 @@
             )
 
         def start(self):
-            peers(lambda p, where: self.copy(p, where, me).start())
+            peers(lambda p, where: self.used(me, p, lambda: self.copy(p, where, me).start()))
+            if self.idle_to >= 0:
+                @pl.when(me == self.idle_to)
+                def _():
+                    self.dst[...] = jnp.zeros_like(self.dst)
+
             if self.src is not None:
                 self.dst[me] = self.src[me]
 
         def wait(self):
-            peers(lambda p, where: self.copy(p, where, p).wait_recv())
+            peers(lambda p, where: self.used(p, me, lambda: self.copy(p, where, p).wait_recv()))
 
         def finish(self):
-            peers(lambda p, where: self.copy(p, where, p).wait_send())
+            peers(lambda p, where: self.used(me, p, lambda: self.copy(p, where, p).wait_send()))
 
     z_ex, w_ex = Exchange(0, None, zb), Exchange(1, None, wb)
-    p_ex, e_ex = Exchange(2, p_out, p_in), Exchange(3, e_out, e_in)
-    a_ex, f_ex = Exchange(4, a_out, a_in), Exchange(5, f_out, f_in)
+    p_ex, e_ex = Exchange(2, p_out, p_in, idle_from=n - 1), Exchange(3, e_out, e_in, idle_to=0)
+    a_ex, f_ex = Exchange(4, a_out, a_in, idle_from=0), Exchange(5, f_out, f_in, idle_to=n - 1)
 
     peers(lambda p, where: pl.semaphore_signal(barrier, inc=1, device_id=where, device_id_type=MESH))
 
@@ -158,14 +172,16 @@
     total = jnp.zeros_like(p_in[0])
     for l in range(n):
         e_out[l] = total
-        total = total + p_in[l]
+        if l < n - 1:
+            total = total + p_in[l]
     e_ex.start()
     fill(FILL[2])
     a_ex.wait()
     total = jnp.zeros_like(a_in[0])
     for l in range(n - 1, -1, -1):
         f_out[l] = total
-        total = total + a_in[l]
+        if l > 0:
+            total = total + a_in[l]
     f_ex.start()
     fill(FILL[3])
     e_ex.wait()

time: 26.6 us -> 25.6 us (0.962)
  Pallas kernels: 25.8 us -> 24.8 us
    pallas_call x1, Pallas kernels: 24.2 us -> 23.3 us  [shards(): pl.pallas_call(functools.partial(kernel, n_o, n_i, heads), out_shape=held...]
where the time goes in v4:
time: 25.6 us; the launch traced here: 25.5 us
  Pallas kernels  24.8 us (97%)
  between operations  0.64 us (2%)
    pallas_call x1, Pallas kernels, shards(): pl.pallas_call(functools.partial(kernel, n_o, n_i, heads), out_shape=held...  23.3 us
    pallas_call x1, Pallas kernels, shards(): pl.pallas_call(functools.partial(closing, heads), out_shape=[array] * 3,...  1.57 us

profile of v4, /device:TPU:0, one launch (start us, length us, event | category | flops | bytes accessed | tf_op | source)
XLA Modules:
  0.0 25.5 jit_solution(9854857687048987448)
XLA Ops:
  0.6 23.3 %shard_map.67 = (f32[384,256]{1,0:T(8,128)S(1)}, f32[384,256]{1,0:T(8,128)S(1)}, f32[384,256]{1,0:T(8,128)S(1)}, f32[384,256]{1,0:T(8,128)S(1)}, f32[384,256]{1,...) custom-call(f32[384,256]{1,0:T(8,128)} %q_hbm.1, f32[384,256]{1,0:T(8,128)} %k_hbm.1, f32[384,256]{1,0:T(8,128)} %v_hbm.1, ...), custom_call_target="tpu_custom_call" | custom-call | tf_op jit(solution)/shard_map/pallas_call | solution.py:243
  23.9 1.6 %shard_map.68 = (f32[384,256]{1,0:T(8,128)}, f32[384,256]{1,0:T(8,128)}, f32[384,256]{1,0:T(8,128)}) custom-call(f32[384,256]{1,0:T(8,128)S(1)} %get-tuple-element.10.gq_ref, f32[384,256]{1,0:T(8,128)S(1)} %get-tuple-element.11.gk_ref, f32[384,256]{1,0:T(8,128)S(1)} %get-tuple-element.12.gv_ref, f32[384,256]{1,0:T(8,128)S(1)} %get-tuple-element.13.fk_ref, ...), custom_call_target="tpu_custom_call" | custom-call | tf_op jit(solution)/shard_map/pallas_call | solution.py:255
